TPU v7x, 32 devices: a whole 2x2x4 slice. The times are simulated.
32 devices in a mesh: groups: 1, rows: 16 (over z, y, core), cols: 2 (over x), sub: 1.
Axes of the slice: x: 2, y: 2, z: 4, core: 2. Of those that a mesh axis runs over, the one named last changes fastest.
Arguments:
- activations: bfloat16 [4096, 5376], P(('groups', 'rows'), ('cols', 'sub')), may hold values from -40 to 40
- positions: int32 [4096], P('groups'), may hold values from 0 to 6143, as said below
- query_weight: bfloat16 [5376, 4096], P('rows', ('cols', 'sub')), may hold values from -0.078125 to 0.078125
- key_weight: bfloat16 [5376, 2048], P('rows', ('cols', 'sub')), may hold values from -0.078125 to 0.078125
- value_weight: bfloat16 [5376, 2048], P('rows', ('cols', 'sub')), may hold values from -0.078125 to 0.078125
- output_weight: bfloat16 [4096, 5376], P(('cols', 'sub'), 'rows'), may hold values from -0.09375 to 0.09375
- input_gain: float32 [5376], replicated, may hold values from 0.1 to 1.9
- query_gain: float32 [128], replicated, may hold values from 0.1 to 1.9
- key_gain: float32 [128], replicated, may hold values from 0.1 to 1.9
Outputs:
- attended: bfloat16 [4096, 5376], P(('groups', 'rows'), ('cols', 'sub'))
Inputs may be any that keep to these rules, and one draw needn't show every extreme that they name: `positions`: position of each token in its document: it rises by one from token to token, or falls to 0 where a new document begins; the first document may begin at any position.
All inputs are finite; a program needn't handle non-finite values.
Results may differ from a plain program's by a relative error of at most 0.0065.
Values may be sent and summed in bfloat16 or wider, within the bound.
A program may use at most 128 MiB of HBM per device.

v0:
```python
import math

import jax
import jax.numpy as jnp
from jax import lax
from jax.sharding import PartitionSpec as P

HD = 128
WINDOW = 1024
QUERY_SCALAR = 168


def passed_along(value, axis, by):
    peers = lax.axis_size(axis)
    pairs = [(i, i + by) for i in range(peers) if 0 <= i + by < peers]
    return lax.ppermute(value, axis, pairs)


def head_norm(tensor, gain_vector):
    return (
        tensor * lax.rsqrt(jnp.mean(tensor * tensor, axis=-1, keepdims=True) + 1e-06) * gain_vector
    )


def rotate(tensor, token_positions):
    half_width = tensor.shape[-1] // 2
    frequency = 10000.0 ** (-(jnp.arange(half_width, dtype=jnp.float32) * 2.0 / tensor.shape[-1]))
    angles = token_positions.astype(jnp.float32)[:, None] * frequency[None, :]
    cosine = jnp.cos(angles)[:, None, :]
    sine_part = jnp.sin(angles)[:, None, :]
    first_half = tensor[..., :half_width]
    second_half = tensor[..., half_width:]
    return jnp.concatenate(
        [
            first_half * cosine - second_half * sine_part,
            second_half * cosine + first_half * sine_part,
        ],
        axis=-1,
    )


def attend(queries, key_rows, value_rows, query_index, key_index, query_pos, key_pos):
    row_count = queries.shape[0]
    key_count = key_rows.shape[0]
    kv_heads = key_rows.shape[1] // HD
    group_size = queries.shape[1] // key_rows.shape[1]
    query_four = queries.reshape(row_count, kv_heads, group_size, HD)
    key_three = key_rows.reshape(key_count, kv_heads, HD)
    value_three = value_rows.reshape(key_count, kv_heads, HD)
    score_scale = 1.0 / math.sqrt(QUERY_SCALAR)
    scores = (
        jnp.einsum("qgrd,kgd->grqk", query_four, key_three, preferred_element_type=jnp.float32)
        * score_scale
    )
    distance = query_index[:, None] - key_index[None, :]
    visible = (
        (key_index[None, :] >= 0)
        & (distance >= 0)
        & (distance < WINDOW)
        & (query_pos[:, None] - key_pos[None, :] == distance)
    )
    weights = jnp.where(visible[None, None], jnp.exp(scores), 0.0)
    totals = jnp.sum(weights, axis=-1)
    rounded = weights.astype(jnp.bfloat16)
    mixed_heads = jnp.einsum(
        "grqk,kgd->qgrd", rounded, value_three, preferred_element_type=jnp.float32
    )
    mixed_heads = mixed_heads / jnp.transpose(totals, (2, 0, 1))[..., None]
    return mixed_heads.astype(jnp.bfloat16).reshape(row_count, kv_heads * group_size * HD)


def reach_back(key_rows, value_rows, reach_rows):
    pieces = []
    carried = (key_rows, value_rows)
    for distance in range(reach_rows):
        carried = passed_along((carried[0], carried[1]), "rows", 1)
        pieces.append(carried)
    ordered = pieces[::-1] + [(key_rows, value_rows)]
    all_keys = jnp.concatenate([member[0] for member in ordered], axis=0)
    all_values = jnp.concatenate([member[1] for member in ordered], axis=0)
    return (all_keys, all_values)


def body(
    activations,
    positions,
    query_weight,
    key_weight,
    value_weight,
    output_weight,
    input_gain,
    query_gain,
    key_gain,
):
    rows_here = activations.shape[0]
    row_panel = lax.all_gather(activations, ("cols", "sub"), axis=1, tiled=True)
    panel_wide = row_panel.astype(jnp.float32)
    inverse = lax.rsqrt(jnp.mean(panel_wide * panel_wide, axis=-1, keepdims=True) + 1e-06)
    normed = (panel_wide * inverse * input_gain).astype(jnp.bfloat16)
    row_index = lax.axis_index("rows")
    own_positions = lax.dynamic_slice_in_dim(positions, row_index * rows_here, rows_here, 0)
    reach_rows = min(-(-WINDOW // rows_here), lax.axis_size("rows") - 1)

    def add_rows(weight_piece):
        return jnp.dot(normed, weight_piece, preferred_element_type=jnp.float32)

    weight_piece = (
        lax.all_gather(query_weight, "rows", axis=0, tiled=True),
        lax.all_gather(key_weight, "rows", axis=0, tiled=True),
        lax.all_gather(value_weight, "rows", axis=0, tiled=True),
    )
    query_raw = add_rows(weight_piece[0])
    key_raw = add_rows(weight_piece[1])
    value_raw = add_rows(weight_piece[2])
    key_rows = rotate(head_norm(key_raw.reshape(rows_here, -1, HD), key_gain), own_positions)
    key_rows, value_rows = (
        key_rows.astype(jnp.bfloat16).reshape(rows_here, -1),
        value_raw.astype(jnp.bfloat16),
    )
    all_keys, all_values = reach_back(key_rows, value_rows, reach_rows)
    queries = rotate(head_norm(query_raw.reshape(rows_here, -1, HD), query_gain), own_positions)
    queries = queries.astype(jnp.bfloat16).reshape(rows_here, -1)
    key_count = all_keys.shape[0]
    query_index = row_index * rows_here + jnp.arange(rows_here, dtype=jnp.int32)
    key_index = (row_index - reach_rows) * rows_here + jnp.arange(key_count, dtype=jnp.int32)
    padded = jnp.concatenate([jnp.zeros((reach_rows * rows_here,), jnp.int32), positions], axis=0)
    key_positions = lax.dynamic_slice_in_dim(padded, row_index * rows_here, key_count, 0)
    context = attend(
        queries, all_keys, all_values, query_index, key_index, own_positions, key_positions
    )
    partial_terms = jnp.dot(
        context,
        lax.all_gather(output_weight, "rows", axis=1, tiled=True),
        preferred_element_type=jnp.float32,
    )
    summed = lax.psum_scatter(
        partial_terms.astype(jnp.bfloat16), ("cols", "sub"), scatter_dimension=1, tiled=True
    ).astype(jnp.float32)
    return (activations.astype(jnp.float32) + summed).astype(jnp.bfloat16)


def solution(mesh):
    placed = (
        P(("groups", "rows"), ("cols", "sub")),
        P("groups"),
        P("rows", ("cols", "sub")),
        P("rows", ("cols", "sub")),
        P("rows", ("cols", "sub")),
        P(("cols", "sub"), "rows"),
        P(),
        P(),
        P(),
    )
    return jax.shard_map(
        body,
        mesh=mesh,
        in_specs=placed,
        out_specs=P(("groups", "rows"), ("cols", "sub")),
        check_vma=False,
    )
```

profile of v0, /device:TPU:0, one launch (start us, length us, event | category | flops | bytes accessed | tf_op | source)
XLA Modules:
  0.0 573.6 jit_solution(11946632752547401691)
XLA Ops:
  10.6 41.5 %all-gather.6.cloned.1.call-done = bf16[256,5376]{1,0:T(8,128)(2,1)} async-done(((bf16[256,2688]{1,0:T(8,128)(2,1)}), bf16[256,5376]{1,0:T(8,128)(2,1)}) %all-gather.6.cloned.1.call-update) | async-done | bytes 2752528 | tf_op jit(solution)/shard_map/all_gather | solution.py:96
  52.1 2.6 fusion.2
  54.7 90.9 %all-gather.8.cloned.1.call-done = bf16[5376,1024]{1,0:T(8,128)(2,1)} async-done(((bf16[336,1024]{1,0:T(8,128)(2,1)}), bf16[5376,1024]{1,0:T(8,128)(2,1)}) %all-gather.8.cloned.1.call-update) | async-done | bytes 11010064 | tf_op jit(solution)/shard_map/all_gather | solution.py:110
  145.6 8.0 %convolution_convert_fusion.1 = bf16[256,1024]{1,0:T(8,128)(2,1)} fusion(bf16[5376,1024]{1,0:T(8,128)(2,1)} %all-gather.8.cloned.1.call-done, bf16[256,5376]{1,0:T(8,128)(2,1)S(1)} %copy-done.1, f32[5376]{0:T(1024)S(1)} %copy-done.8, f32[256]{0:T(256)S(1)} %add_rsqrt_fusion.2), kind=kOutput, calls=%fused_computation.24 | convolution fusion | flops 2824339456 | bytes 14309376 | tf_op jit(solution)/shard_map/dot_general | solution.py:105
  153.5 2.2 collective-permute-start
  155.7 87.0 %all-gather.10.cloned.1.call-done = bf16[5376,1024]{1,0:T(8,128)(2,1)} async-done(((bf16[336,1024]{1,0:T(8,128)(2,1)}), bf16[5376,1024]{1,0:T(8,128)(2,1)}) %all-gather.10.cloned.1.call-update) | async-done | bytes 11010064 | tf_op jit(solution)/shard_map/all_gather | solution.py:109
  242.7 6.7 %fusion.18 = f32[256,1024]{1,0:T(8,128)S(1)} fusion(bf16[5376,1024]{1,0:T(8,128)(2,1)} %all-gather.10.cloned.1.call-done, bf16[256,5376]{1,0:T(8,128)(2,1)} %all-gather.6.cloned.1.call-done, f32[5376]{0:T(1024)S(1)} %copy-done.8, f32[256]{0:T(256)S(1)} %add_rsqrt_fusion.2), kind=kOutput, calls=%fused_computation.55 | convolution fusion | flops 2824077312 | bytes 14833664 | tf_op jit(solution)/shard_map/dot_general | solution.py:105
  251.4 2.2 collective-permute-start.4
  253.6 2.3 collective-permute-start.1
  255.9 17.3 %collective-permute-start.5 = (bf16[256,1024]{0,1:T(8,128)(2,1)S(1)}, bf16[256,1024]{0,1:T(8,128)(2,1)S(1)}, u32[]{:S(2)}, u32[]{:S(2)}) collective-permute-start(bf16[256,1024]{0,1:T(8,128)(2,1)S(1)} %collective-permute-done.4), channel_id=1, source_target_pairs={{0,2},{2,4},{4,6},{6,8},{8,10},{10,12},{12,14},{14,16},{16,18},{18... | collective-permute-start | bytes 1572872 | tf_op jit(solution)/shard_map/ppermute | solution.py:16
  273.2 17.6 %collective-permute-start.2 = (bf16[256,1024]{1,0:T(8,128)(2,1)S(1)}, bf16[256,1024]{1,0:T(8,128)(2,1)}, u32[]{:S(2)}, u32[]{:S(2)}) collective-permute-start(bf16[256,1024]{1,0:T(8,128)(2,1)S(1)} %collective-permute-done.1), channel_id=1, source_target_pairs={{0,2},{2,4},{4,6},{6,8},{8,10},{10,12},{12,14},{14,16},{16,18},{18... | collective-permute-start | bytes 1572872 | tf_op jit(solution)/shard_map/ppermute | solution.py:16
  290.9 16.8 %collective-permute-start.6 = (bf16[256,1024]{0,1:T(8,128)(2,1)S(1)}, bf16[256,1024]{0,1:T(8,128)(2,1)}, u32[]{:S(2)}, u32[]{:S(2)}) collective-permute-start(bf16[256,1024]{0,1:T(8,128)(2,1)S(1)} %collective-permute-done.5), channel_id=1, source_target_pairs={{0,2},{2,4},{4,6},{6,8},{8,10},{10,12},{12,14},{14,16},{16,18},{18... | collective-permute-start | bytes 1572872 | tf_op jit(solution)/shard_map/ppermute | solution.py:16
  307.7 16.8 %collective-permute-start.3 = (bf16[256,1024]{1,0:T(8,128)(2,1)}, bf16[256,1024]{1,0:T(8,128)(2,1)}, u32[]{:S(2)}, u32[]{:S(2)}) collective-permute-start(bf16[256,1024]{1,0:T(8,128)(2,1)} %collective-permute-done.2), channel_id=1, source_target_pairs={{0,2},{2,4},{4,6},{6,8},{8,10},{10,12},{12,14},{14,16},{16,18},{18... | collective-permute-start | bytes 1572872 | tf_op jit(solution)/shard_map/ppermute | solution.py:16
  324.6 2.0 fusion.9
  327.2 1.3 copy.52
  328.5 14.2 %collective-permute-start.7 = (bf16[256,1024]{0,1:T(8,128)(2,1)}, bf16[256,1024]{0,1:T(8,128)(2,1)}, u32[]{:S(2)}, u32[]{:S(2)}) collective-permute-start(bf16[256,1024]{0,1:T(8,128)(2,1)} %collective-permute-done.6), channel_id=1, source_target_pairs={{0,2},{2,4},{4,6},{6,8},{8,10},{10,12},{12,14},{14,16},{16,18},{18... | collective-permute-start | bytes 1572872 | tf_op jit(solution)/shard_map/ppermute | solution.py:16
  342.7 1.9 constant_dynamic-update-slice_fusion.4
  344.6 1.9 constant_dynamic-update-slice_fusion.3
  346.5 1.9 constant_dynamic-update-slice_fusion.2
  349.2 1.9 constant_dynamic-update-slice_fusion
  351.1 4.5 copy.64
  355.6 1.3 copy.51
  361.6 29.8 %all-gather.12.cloned.1.call-done = bf16[5376,2048]{1,0:T(8,128)(2,1)} async-done(((bf16[336,2048]{1,0:T(8,128)(2,1)}), bf16[5376,2048]{1,0:T(8,128)(2,1)}) %all-gather.12.cloned.1.call-update) | async-done | bytes 22020112 | tf_op jit(solution)/shard_map/all_gather | solution.py:108
  391.4 11.1 %convolution_bitcast_fusion = f32[32,8,16,128]{3,1,2,0:T(8,128)S(1)} fusion(bf16[5376,2048]{1,0:T(8,128)(2,1)} %all-gather.12.cloned.1.call-done, bf16[256,5376]{1,0:T(8,128)(2,1)} %all-gather.6.cloned.1.call-done, f32[5376]{0:T(1024)S(1)} %copy-done.8, f32[256]{0:T(256)S(1)} %add_rsqrt_fusion.2), kind=kOutput, calls=%fused_computation.20 | convolution fusion | flops 5642649600 | bytes 26892288 | tf_op jit(solution)/shard_map/dot_general | solution.py:105
  406.4 7.6 %fusion.22 = (f32[8,2,256]{2,1,0:T(2,128)S(1)}, bf16[8,2,256,1280]{2,3,1,0:T(8,128)(2,1)S(1)}) fusion(bf16[256,8,2,64]{3,0,2,1:T(8,128)(2,1)S(1)} %bitcast.55, bf16[256,8,2,64]{3,0,2,1:T(8,128)(2,1)S(1)} %bitcast.56, bf16[1280,8,128]{2,0,1:T(8,128)(2,1)} %constant_dynamic-update-slice_fusion.5, pred[256,1280]{0,1:T(8,128)(4,1)S(1)} %copy-done.4), kind=kOutput, calls=%fused_computation.57 | convolution fusion | flops 1365241856 | bytes 14499840 | tf_op jit(solution)/shard_map/qgrd,kgd->grqk/dot_general | solution.py:52
  414.0 2.5 fusion.6
  416.5 94.2 %all-gather.14.cloned.1.call-done = bf16[2048,5376]{0,1:T(8,128)(2,1)} async-done(((bf16[2048,336]{0,1:T(8,128)(2,1)}), bf16[2048,5376]{0,1:T(8,128)(2,1)}) %all-gather.14.cloned.1.call-update) | async-done | bytes 22020112 | tf_op jit(solution)/shard_map/all_gather | solution.py:133
  510.7 10.8 %convolution_convert_fusion = bf16[256,5376]{1,0:T(8,128)(2,1)S(1)} fusion(bf16[256,2048]{0,1:T(8,128)(2,1)} %bitcast.60, bf16[2048,5376]{0,1:T(8,128)(2,1)} %all-gather.14.cloned.1.call-done), kind=kOutput, calls=%fused_computation.3 | convolution fusion | flops 5638520832 | bytes 25821184 | tf_op jit(solution)/shard_map/dot_general | solution.py:131
  521.5 2.8 copy.65
  524.3 39.2 %reduce-scatter.4.cloned.1.call-done = bf16[2688,256]{1,0:T(8,128)(2,1)} async-done(((bf16[5376,256]{1,0:T(8,128)(2,1)}), bf16[2688,256]{1,0:T(8,128)(2,1)}) %reduce-scatter.4.cloned.1.call-update) | async-done | bytes 1376272
  563.5 1.8 copy.66
  565.3 1.4 add_convert_fusion
  (69 shorter events, 15.8 us)
Async XLA Ops:
  6.5 3.5 copy-start.5
  6.5 45.6 %all-gather.6.cloned.1.call-start = ((), (), s32[]{:S(2)}) async-start(), calls=%async_computation.1 | async-start | bytes 4128768 | tf_op jit(solution)/shard_map/all_gather | solution.py:96
  7.3 138.3 %all-gather.8.cloned.1.call-start = ((), (), s32[]{:S(2)}) async-start(), calls=%async_computation.2 | async-start | bytes 11698176 | tf_op jit(solution)/shard_map/all_gather | solution.py:110
  8.0 234.7 %all-gather.10.cloned.1.call-start = ((), (), s32[]{:S(2)}) async-start(), calls=%async_computation.3 | async-start | bytes 11698176 | tf_op jit(solution)/shard_map/all_gather | solution.py:109
  8.7 136.8 %copy-start.8 = (f32[5376]{0:T(1024)S(1)}, f32[5376]{0:T(1024)}, u32[]{:S(2)}) copy-start(f32[5376]{0:T(1024)} %param.15) | copy-start | bytes 64516
  8.8 382.7 %all-gather.12.cloned.1.call-start = ((), (), s32[]{:S(2)}) async-start(), calls=%async_computation.4 | async-start | bytes 23396352 | tf_op jit(solution)/shard_map/all_gather | solution.py:108
  9.3 501.4 %all-gather.14.cloned.1.call-start = ((), (), s32[]{:S(2)}) async-start(), calls=%async_computation.5 | async-start | bytes 23396352 | tf_op jit(solution)/shard_map/all_gather | solution.py:133
  9.9 553.6 %reduce-scatter.4.cloned.1.call-start = ((), (), s32[]{:S(2)}) async-start(), calls=%async_computation.6 | async-start | bytes 4128768
  52.1 93.4 %copy-start.1 = (bf16[256,5376]{1,0:T(8,128)(2,1)S(1)}, bf16[256,5376]{1,0:T(8,128)(2,1)}, u32[]{:S(2)}) copy-start(bf16[256,5376]{1,0:T(8,128)(2,1)} %all-gather.6.cloned.1.call-done) | copy-start | bytes 8257540
  153.5 100.0 %collective-permute-start = (bf16[256,1024]{1,0:T(8,128)(2,1)}, bf16[256,1024]{1,0:T(8,128)(2,1)S(1)}, u32[]{:S(2)}, u32[]{:S(2)}) collective-permute-start(bf16[256,1024]{1,0:T(8,128)(2,1)} %convolution_convert_fusion.1), channel_id=1, source_target_pairs={{0,2},{2,4},{4,6},{6,8},{8,10},{10,12},{12,14},{14,16},{16,18},{18... | collective-permute-start | bytes 1572872 | tf_op jit(solution)/shard_map/ppermute | solution.py:16
  249.4 0.7 copy-start.6
  251.4 4.6 collective-permute-start.4
  253.6 19.6 %collective-permute-start.1 = (bf16[256,1024]{1,0:T(8,128)(2,1)S(1)}, bf16[256,1024]{1,0:T(8,128)(2,1)S(1)}, u32[]{:S(2)}, u32[]{:S(2)}) collective-permute-start(bf16[256,1024]{1,0:T(8,128)(2,1)S(1)} %collective-permute-done), channel_id=1, source_target_pairs={{0,2},{2,4},{4,6},{6,8},{8,10},{10,12},{12,14},{14,16},{16,18},{18... | collective-permute-start | bytes 1572872 | tf_op jit(solution)/shard_map/ppermute | solution.py:16
  255.9 35.0 %collective-permute-start.5 = (bf16[256,1024]{0,1:T(8,128)(2,1)S(1)}, bf16[256,1024]{0,1:T(8,128)(2,1)S(1)}, u32[]{:S(2)}, u32[]{:S(2)}) collective-permute-start(bf16[256,1024]{0,1:T(8,128)(2,1)S(1)} %collective-permute-done.4), channel_id=1, source_target_pairs={{0,2},{2,4},{4,6},{6,8},{8,10},{10,12},{12,14},{14,16},{16,18},{18... | collective-permute-start | bytes 1572872 | tf_op jit(solution)/shard_map/ppermute | solution.py:16
  273.2 53.4 %copy-start.3 = (bf16[256,1024]{1,0:T(8,128)(2,1)}, bf16[256,1024]{1,0:T(8,128)(2,1)S(1)}, u32[]{:S(2)}) copy-start(bf16[256,1024]{1,0:T(8,128)(2,1)S(1)} %collective-permute-done.1) | copy-start | bytes 1572868
  273.2 34.5 %collective-permute-start.2 = (bf16[256,1024]{1,0:T(8,128)(2,1)S(1)}, bf16[256,1024]{1,0:T(8,128)(2,1)}, u32[]{:S(2)}, u32[]{:S(2)}) collective-permute-start(bf16[256,1024]{1,0:T(8,128)(2,1)S(1)} %collective-permute-done.1), channel_id=1, source_target_pairs={{0,2},{2,4},{4,6},{6,8},{8,10},{10,12},{12,14},{14,16},{16,18},{18... | collective-permute-start | bytes 1572872 | tf_op jit(solution)/shard_map/ppermute | solution.py:16
  290.9 36.2 %collective-permute-start.6 = (bf16[256,1024]{0,1:T(8,128)(2,1)S(1)}, bf16[256,1024]{0,1:T(8,128)(2,1)}, u32[]{:S(2)}, u32[]{:S(2)}) collective-permute-start(bf16[256,1024]{0,1:T(8,128)(2,1)S(1)} %collective-permute-done.5), channel_id=1, source_target_pairs={{0,2},{2,4},{4,6},{6,8},{8,10},{10,12},{12,14},{14,16},{16,18},{18... | collective-permute-start | bytes 1572872 | tf_op jit(solution)/shard_map/ppermute | solution.py:16
  307.7 35.0 %collective-permute-start.3 = (bf16[256,1024]{1,0:T(8,128)(2,1)}, bf16[256,1024]{1,0:T(8,128)(2,1)}, u32[]{:S(2)}, u32[]{:S(2)}) collective-permute-start(bf16[256,1024]{1,0:T(8,128)(2,1)} %collective-permute-done.2), channel_id=1, source_target_pairs={{0,2},{2,4},{4,6},{6,8},{8,10},{10,12},{12,14},{14,16},{16,18},{18... | collective-permute-start | bytes 1572872 | tf_op jit(solution)/shard_map/ppermute | solution.py:16
  328.5 27.1 %collective-permute-start.7 = (bf16[256,1024]{0,1:T(8,128)(2,1)}, bf16[256,1024]{0,1:T(8,128)(2,1)}, u32[]{:S(2)}, u32[]{:S(2)}) collective-permute-start(bf16[256,1024]{0,1:T(8,128)(2,1)} %collective-permute-done.6), channel_id=1, source_target_pairs={{0,2},{2,4},{4,6},{6,8},{8,10},{10,12},{12,14},{14,16},{16,18},{18... | collective-permute-start | bytes 1572872 | tf_op jit(solution)/shard_map/ppermute | solution.py:16
  402.5 1.2 copy-start.7
  405.4 1.0 copy-start.4
  406.4 7.6 %copy-start.2 = (bf16[1280,1024]{0,1:T(8,128)(2,1)S(1)}, bf16[1280,1024]{0,1:T(8,128)(2,1)}, u32[]{:S(2)}) copy-start(bf16[1280,1024]{0,1:T(8,128)(2,1)} %copy.64) | copy-start | bytes 7864324
  524.3 41.0 %copy-start = (bf16[256,2688]{1,0:T(8,128)(2,1)S(1)}, bf16[256,2688]{1,0:T(8,128)(2,1)}, u32[]{:S(2)}) copy-start(bf16[256,2688]{1,0:T(8,128)(2,1)} %param.9) | copy-start | bytes 4128772
Sparse Core Ops, SparseCore 0:
  8.9 43.1 all-gather.5
  54.4 91.0 all-gather.7
  147.8 94.7 all-gather.9
  244.1 147.2 all-gather.11
  392.9 117.7 all-gather.13
  524.4 39.0 reduce-scatter.3
where the time goes:
time: 574 us
  waiting for transfers between devices  386 us (67%)
  starting transfers between devices  89.6 us (16%)
  matrix products  46.7 us (8%)
  local copies, waits for them, and re-layouts  26.3 us (5%)
  between operations  13.8 us (2%)
  other arithmetic  11.4 us (2%)
    all_gather x1, waiting for transfers between devices, body(): lax.all_gather(output_weight, 'rows', axis=1, tiled=True)  94.2 us
    all_gather x1, waiting for transfers between devices, body(): lax.all_gather(value_weight, 'rows', axis=0, tiled=True)  90.9 us
    ppermute x8, starting transfers between devices, passed_along(): return lax.ppermute(value, axis, pairs)  89.5 us
    all_gather x1, waiting for transfers between devices, body(): lax.all_gather(key_weight, 'rows', axis=0, tiled=True)  87 us
    unnamed x7, waiting for transfers between devices  42.4 us
    all_gather x1, waiting for transfers between devices, body(): row_panel = lax.all_gather(activations, ('cols', 'sub'), axis=1, tiled=True)  41.5 us
    all_gather x1, waiting for transfers between devices, body(): lax.all_gather(query_weight, 'rows', axis=0, tiled=True)  29.8 us
    dot_general x3, matrix products, add_rows(): return jnp.dot(normed, weight_piece, preferred_element_type=jnp.float32)  25.8 us
  transfers between devices with their start and end apart: 14, of which 6 were waited for; matrix products, arithmetic and copies ran while one was open for 12% of the time, Pallas kernels for 0%

commit v1 on v0

--- a/solution.py
+++ b/solution.py
@@ -1,8 +1,12 @@
+import functools
 import math
 
 import jax
 import jax.numpy as jnp
 from jax import lax
+from jax.experimental import pallas as pl
+from jax.experimental.pallas import tpu as pltpu
+from jax.sharding import Mesh
 from jax.sharding import PartitionSpec as P
 
 HD = 128
@@ -139,7 +143,7 @@
     return (activations.astype(jnp.float32) + summed).astype(jnp.bfloat16)
 
 
-def solution(mesh):
+def row_solution(mesh):
     placed = (
         P(("groups", "rows"), ("cols", "sub")),
         P("groups"),
@@ -158,3 +162,339 @@
         out_specs=P(("groups", "rows"), ("cols", "sub")),
         check_vma=False,
     )
+
+def flipped(value, axis):
+    return lax.ppermute(value, axis, [(0, 1), (1, 0)])
+
+
+def pick(array, index, axis):
+    return lax.dynamic_index_in_dim(array, index, axis, keepdims=False)
+
+
+def reduce_in_plane(terms, width_here):
+    rows = terms.shape[0] // 4
+    mid, low, col = lax.axis_index("mid"), lax.axis_index("low"), lax.axis_index("cols")
+    four = terms.reshape(2, 2, rows, -1)
+    got = flipped(pick(four, 1 - low, 1), "low")
+    chip = (pick(four, low, 1).astype(jnp.float32) + got.astype(jnp.float32)).astype(jnp.bfloat16)
+
+    def columns(array, index):
+        return lax.dynamic_slice_in_dim(array, index * width_here, width_here, array.ndim - 1)
+
+    def added(a, b):
+        return a.astype(jnp.float32) + b.astype(jnp.float32)
+
+    first, second = chip[:, : rows // 2], chip[:, rows // 2 :]
+    got_a = flipped(columns(first, 1 - col), "cols")
+    got_b = flipped(pick(second, 1 - mid, 0), "mid")
+    part_a = added(columns(first, col), got_a).astype(jnp.bfloat16)
+    part_b = added(pick(second, mid, 0), got_b).astype(jnp.bfloat16)
+    got_a = flipped(pick(part_a, 1 - mid, 0), "mid")
+    got_b = flipped(columns(part_b, 1 - col), "cols")
+    return jnp.concatenate(
+        [added(pick(part_a, mid, 0), got_a), added(columns(part_b, col), got_b)], axis=0
+    )
+
+
+def gather_kernel(planes, count, *refs):
+    weights, tokens = refs[:count], refs[count]
+    fulls, panel = refs[count + 1 : 2 * count + 1], refs[2 * count + 1]
+    (own_sem, deal_send, deal_recv, up_send, up_recv, down_send, down_recv) = refs[
+        2 * count + 2 : 2 * count + 9
+    ]
+    act_own, act_send, act_recv = refs[2 * count + 9 :]
+    own = lax.axis_index("outer")
+    mid, low, col = lax.axis_index("mid"), lax.axis_index("low"), lax.axis_index("cols")
+    mids, lows, sides = (mid, 1 - mid), (low, 1 - low), (col, 1 - col)
+    depth = weights[0].shape[0]
+    rows = tokens.shape[0]
+    has_up, has_down = own < planes - 1, own > 0
+
+    def plane_peer(k):
+        return {"mid": mids[k // 2], "low": lows[k % 2]}
+
+    def place(k):
+        return mids[k // 2] * 2 + lows[k % 2]
+
+    barrier = pltpu.get_barrier_semaphore()
+    for k in range(8):
+        if k:
+            pl.semaphore_signal(
+                barrier,
+                inc=1,
+                device_id=dict(plane_peer(k % 4), cols=sides[k // 4]),
+                device_id_type=pl.DeviceIdType.MESH,
+            )
+
+    @pl.when(has_up)
+    def _():
+        pl.semaphore_signal(
+            barrier, inc=1, device_id={"outer": own + 1}, device_id_type=pl.DeviceIdType.MESH
+        )
+
+    @pl.when(has_down)
+    def _():
+        pl.semaphore_signal(
+            barrier, inc=1, device_id={"outer": own - 1}, device_id_type=pl.DeviceIdType.MESH
+        )
+
+    pl.semaphore_wait(barrier, 7 + jnp.where(has_up, 1, 0) + jnp.where(has_down, 1, 0))
+
+    def block(t, plane, k):
+        at = pl.multiple_of((plane * 4 + place(k)) * depth, 16)
+        return fulls[t].at[pl.ds(at, depth), :]
+
+    def own_block(t):
+        at = pl.multiple_of((own * 4 + mid * 2 + low) * depth, 16)
+        return fulls[t].at[pl.ds(at, depth), :]
+
+    def part(t, k):
+        wide = fulls[t].shape[1]
+        return weights[t].at[:, pl.ds(pl.multiple_of(place(k) * wide, 128), wide)]
+
+    def local(t):
+        return pltpu.make_async_copy(part(t, 0), own_block(t), own_sem.at[t])
+
+    def deal(t, k):
+        return pltpu.make_async_remote_copy(
+            src_ref=part(t, k),
+            dst_ref=own_block(t),
+            send_sem=deal_send.at[t, k],
+            recv_sem=deal_recv.at[t, k],
+            device_id=plane_peer(k),
+            device_id_type=pl.DeviceIdType.MESH,
+        )
+
+    def passed(t, d, k, step, sends, recvs):
+        where = block(t, jnp.clip(own - step * d, 0, planes - 1), k)
+        return pltpu.make_async_remote_copy(
+            src_ref=where,
+            dst_ref=where,
+            send_sem=sends.at[t, d, k],
+            recv_sem=recvs.at[t, d, k],
+            device_id={"outer": jnp.clip(own + step, 0, planes - 1)},
+            device_id_type=pl.DeviceIdType.MESH,
+        )
+
+    def up(t, d, k):
+        return passed(t, d, k, 1, up_send, up_recv)
+
+    def down(t, d, k):
+        return passed(t, d, k, -1, down_send, down_recv)
+
+    def share(k):
+        at = pl.multiple_of((mid * 2 + low) * rows, 16)
+        where = panel.at[col, pl.ds(at, rows), :]
+        if k == 0:
+            return pltpu.make_async_copy(tokens, where, act_own.at[0])
+        return pltpu.make_async_remote_copy(
+            src_ref=tokens,
+            dst_ref=where,
+            send_sem=act_send.at[k],
+            recv_sem=act_recv.at[k],
+            device_id=dict(plane_peer(k % 4), cols=sides[k // 4]),
+            device_id_type=pl.DeviceIdType.MESH,
+        )
+
+    for t in range(count):
+        local(t).start()
+    for k in (2, 3, 1):
+        for t in range(count):
+            deal(t, k).start()
+    for d in range(planes):
+        for k in (0, 1, 2, 3):
+            for t in range(count):
+                if d == 0:
+                    if k == 0:
+                        local(t).wait()
+                    else:
+                        deal(t, k).wait_recv()
+                if d > 0:
+
+                    @pl.when(own - d >= 0)
+                    def _():
+                        up(t, d - 1, k).wait_recv()
+
+                    @pl.when(own + d < planes)
+                    def _():
+                        down(t, d - 1, k).wait_recv()
+
+                if d < planes - 1:
+
+                    @pl.when((own - d >= 0) & has_up)
+                    def _():
+                        up(t, d, k).start()
+
+                    @pl.when((own + d < planes) & has_down)
+                    def _():
+                        down(t, d, k).start()
+
+        if d == 0:
+            for k in (4, 5, 6, 7, 2, 3, 1, 0):
+                share(k).start()
+    for d in range(planes - 1):
+        for k in range(4):
+            for t in range(count):
+
+                @pl.when((own - d >= 0) & has_up)
+                def _():
+                    up(t, d, k).wait_send()
+
+                @pl.when((own + d < planes) & has_down)
+                def _():
+                    down(t, d, k).wait_send()
+
+    for k in (1, 2, 3):
+        for t in range(count):
+            deal(t, k).wait_send()
+    share(0).wait()
+    for k in range(1, 8):
+        share(k).wait()
+
+
+def gather_all(weights, tokens):
+    planes = lax.axis_size("outer")
+    count = len(weights)
+    depth = weights[0].shape[0]
+    anywhere = pl.BlockSpec(memory_space=pl.ANY)
+    line = pltpu.SemaphoreType.DMA((count, planes - 1, 4))
+    shapes = [
+        jax.ShapeDtypeStruct((planes * 4 * depth, weight.shape[1] // 4), weight.dtype)
+        for weight in weights
+    ]
+    shapes.append(jax.ShapeDtypeStruct((2, 4 * tokens.shape[0], tokens.shape[1]), tokens.dtype))
+    return pl.pallas_call(
+        functools.partial(gather_kernel, planes, count),
+        out_shape=shapes,
+        in_specs=[anywhere] * (count + 1),
+        out_specs=[anywhere] * (count + 1),
+        scratch_shapes=[
+            pltpu.SemaphoreType.DMA((count,)),
+            pltpu.SemaphoreType.DMA((count, 4)),
+            pltpu.SemaphoreType.DMA((count, 4)),
+            line,
+            line,
+            line,
+            line,
+            pltpu.SemaphoreType.DMA((1,)),
+            pltpu.SemaphoreType.DMA((8,)),
+            pltpu.SemaphoreType.DMA((8,)),
+        ],
+        compiler_params=pltpu.CompilerParams(collective_id=0, has_side_effects=True),
+        cost_estimate=pl.CostEstimate(
+            flops=200_000_000_000, bytes_accessed=600_000_000, transcendentals=0
+        ),
+        name="gather_weights",
+    )(*weights, tokens)
+
+
+def plane_body(
+    activations,
+    positions,
+    query_weight,
+    key_weight,
+    value_weight,
+    output_weight,
+    input_gain,
+    query_gain,
+    key_gain,
+):
+    rows_here, width_here = activations.shape
+    inner = 4
+    plane_tokens = inner * rows_here
+    key_full, value_full, query_full, output_full, panel = gather_all(
+        [key_weight, value_weight, query_weight, output_weight.T], activations
+    )
+    left, right = panel[0].astype(jnp.float32), panel[1].astype(jnp.float32)
+    squares = jnp.sum(left * left, axis=-1) + jnp.sum(right * right, axis=-1)
+    inverse = lax.rsqrt(squares[:, None] / (2 * width_here) + 1e-06)
+    normed_left = (left * inverse * input_gain[:width_here]).astype(jnp.bfloat16)
+    normed_right = (right * inverse * input_gain[width_here:]).astype(jnp.bfloat16)
+    outer_index = lax.axis_index("outer")
+    first = outer_index * plane_tokens
+    own_positions = lax.dynamic_slice_in_dim(positions, first, plane_tokens, 0)
+
+    def project(weight):
+        return jnp.dot(
+            normed_left, weight[:width_here], preferred_element_type=jnp.float32
+        ) + jnp.dot(normed_right, weight[width_here:], preferred_element_type=jnp.float32)
+
+    key_raw = project(key_full)
+    keys = rotate(head_norm(key_raw.reshape(plane_tokens, -1, HD), key_gain), own_positions)
+    keys = keys.astype(jnp.bfloat16).reshape(plane_tokens, -1)
+    keys_before = passed_along(keys[plane_tokens - WINDOW :], "outer", 1)
+    values = project(value_full).astype(jnp.bfloat16)
+    values_before = passed_along(values[plane_tokens - WINDOW :], "outer", 1)
+    all_keys = jnp.concatenate([keys_before, keys], axis=0)
+    all_values = jnp.concatenate([values_before, values], axis=0)
+    queries = rotate(
+        head_norm(project(query_full).reshape(plane_tokens, -1, HD), query_gain), own_positions
+    )
+    queries = queries.astype(jnp.bfloat16).reshape(plane_tokens, -1)
+    padded = jnp.concatenate([jnp.zeros((WINDOW,), jnp.int32), positions], axis=0)
+    key_positions = lax.dynamic_slice_in_dim(padded, first, plane_tokens + WINDOW, 0)
+    count = rows_here + WINDOW
+    contexts = []
+    for block in range(inner):
+        at = block * rows_here
+        contexts.append(
+            attend(
+                queries[at : at + rows_here],
+                all_keys[at : at + count],
+                all_values[at : at + count],
+                first + at + jnp.arange(rows_here, dtype=jnp.int32),
+                first + at - WINDOW + jnp.arange(count, dtype=jnp.int32),
+                own_positions[at : at + rows_here],
+                key_positions[at : at + count],
+            )
+        )
+    context = jnp.concatenate(contexts, axis=0)
+    terms = lax.dot_general(
+        context, output_full, (((1,), (1,)), ((), ())), preferred_element_type=jnp.float32
+    ).astype(jnp.bfloat16)
+    summed = reduce_in_plane(terms, width_here)
+    return (activations.astype(jnp.float32) + summed).astype(jnp.bfloat16)
+
+
+def plane_solution(mesh):
+    sizes = mesh.shape
+    split = Mesh(
+        mesh.devices.reshape(
+            sizes["groups"], sizes["rows"] // 4, 2, 2, sizes["cols"], sizes["sub"]
+        ),
+        ("groups", "outer", "mid", "low", "cols", "sub"),
+    )
+    rows, cols = ("outer", "mid", "low"), ("cols", "sub")
+    placed = (
+        P(("groups",) + rows, cols),
+        P("groups"),
+        P(rows, cols),
+        P(rows, cols),
+        P(rows, cols),
+        P(cols, rows),
+        P(),
+        P(),
+        P(),
+    )
+    return jax.shard_map(
+        plane_body,
+        mesh=split,
+        in_specs=placed,
+        out_specs=P(("groups",) + rows, cols),
+        check_vma=False,
+    )
+
+
+def solution(mesh):
+    sizes = mesh.shape
+    parts = sizes["cols"] * sizes["sub"]
+
+    def run(*args):
+        tokens = args[0].shape[0] // (sizes["groups"] * sizes["rows"])
+        kv_heads = args[3].shape[1] // (HD * parts)
+        fits = sizes["rows"] % (4 * parts) == 0 and kv_heads % 4 == 0
+        fits = fits and sizes["cols"] == 2 and sizes["sub"] == 1 and tokens * 4 >= WINDOW
+        plan = plane_solution(mesh) if fits else row_solution(mesh)
+        return plan(*args)
+
+    return run

time: 574 us -> 450 us (0.78)
  waiting for transfers between devices: 386 us -> 54.4 us
  Pallas kernels: 0 us -> 292 us
  starting transfers between devices: 89.6 us -> 9.13 us
  other arithmetic: 11.4 us -> 37.7 us
  between operations: 13.8 us -> 0.66 us
  local copies, waits for them, and re-layouts: 26.3 us -> 16.2 us
  matrix products: 46.7 us -> 39.6 us
    all_gather x5 -> x0, waiting for transfers between devices: 343 us -> none  [the longest x1 94.2 us: body(): lax.all_gather(output_weight, 'rows', axis=1, tiled=True)]
    pallas_call x0 -> x1, Pallas kernels: none -> 292 us  [gather_all(): pl.pallas_call(functools.partial(gather_kernel, planes, count), out_shape...]
    ppermute x8 -> x2, starting transfers between devices: 89.5 us -> 5.92 us  [passed_along(): return lax.ppermute(value, axis, pairs)]
    ppermute x0 -> x5, waiting for transfers between devices: none -> 54.4 us  [flipped(): return lax.ppermute(value, axis, [(0, 1), (1, 0)])]
    unnamed x7 -> x0, waiting for transfers between devices: 42.4 us -> none
    convert_element_type x2 -> x5, other arithmetic: 1.69 us -> 16.8 us  [the longest x1 6.35 us: plane_body(): (left * inverse * input_gain[:width_here]).astype(jnp.bfloat16)]
    unnamed x30 -> x50, local copies, waits for them, and re-layouts: 15.7 us -> 8.43 us
    dot_general x4 -> x7, matrix products: 36.6 us -> 31 us  [the longest x3 11 us: project(): jnp.dot(normed_right, weight[width_here:], preferred_element_type=jnp.flo...]
  transfers between devices with their start and end apart: 14 -> 7, of which waited for: 6 -> 4; matrix products, arithmetic and copies ran while one was open for 12% -> 8% of each run, Pallas kernels for 0% -> 0%
where the time goes in v1:
time: 450 us
  Pallas kernels  292 us (65%)
  waiting for transfers between devices  54.4 us (12%)
  matrix products  39.6 us (9%)
  other arithmetic  37.7 us (8%)
  local copies, waits for them, and re-layouts  16.2 us (4%)
  starting transfers between devices  9.13 us (2%)
    pallas_call x1, Pallas kernels, gather_all(): pl.pallas_call(functools.partial(gather_kernel, planes, count), out_shape...  292 us
    ppermute x5, waiting for transfers between devices, flipped(): return lax.ppermute(value, axis, [(0, 1), (1, 0)])  54.4 us
    dot_general x3, matrix products, project(): jnp.dot(normed_right, weight[width_here:], preferred_element_type=jnp.flo...  11 us
    dot_general x3, matrix products, project(): jnp.dot(normed_left, weight[:width_here], preferred_element_type=jnp.floa...  10.5 us
    dot_general x1, matrix products, plane_body(): lax.dot_general(context, output_full, (((1,), (1,)), ((), ())), preferred...  9.41 us
  transfers between devices with their start and end apart: 7, of which 4 were waited for; matrix products, arithmetic and copies ran while one was open for 8% of the time, Pallas kernels for 0%

profile of v1, /device:TPU:0, one launch (start us, length us, event | category | flops | bytes accessed | tf_op | source)
XLA Modules:
  0.0 449.9 jit_solution(9408791793698918584)
XLA Ops:
  0.5 292.2 %gather_weights.1 = (bf16[5376,256]{1,0:T(8,128)(2,1)}, bf16[5376,256]{1,0:T(8,128)(2,1)}, bf16[5376,512]{1,0:T(8,128)(2,1)}, bf16[5376,512]{1,0:T(8,128)(2,1)}, bf16[2,1024,2688]{2,1,0:T(8,128)(2,1)}) custom-call(bf16[336,1024]{1,0:T(8,128)(2,1)} %refs_0_.1, bf16[336,1024]{1,0:T(8,128)(2,1)} %refs_1_.1, bf16[336,2048]{1,0:T(8,128)(2,1)} %refs_2_.1, ...), custom_call_target="tpu_custom_call" | custom-call | flops 199999995904 | bytes 600000000 | tf_op jit(solution)/shard_map/gather_weights/pallas_call | solution.py:366
  292.7 5.8 %fusion.3 = (f32[1024]{0:T(1024)S(1)}, f32[1024]{0:T(1024)S(1)}) fusion(bf16[2,1024,2688]{2,1,0:T(8,128)(2,1)} %get-tuple-element.10), kind=kLoop, calls=%fused_computation.8 | loop fusion | flops 16513024 | bytes 11018240 | tf_op jit(solution)/shard_map/reduce_sum | solution.py:409
  298.6 6.3 %fusion.2 = (bf16[1024,2688]{1,0:T(8,128)(2,1)S(1)}, bf16[1024,2688]{1,0:T(8,128)(2,1)S(1)}) fusion(f32[2688]{0:T(1024)S(1)} %get-tuple-element.39, f32[1024]{0:T(1024)S(1)} %add_rsqrt_fusion.2, bf16[2,1024,2688]{2,1,0:T(8,128)(2,1)} %get-tuple-element.10, f32[2688]{0:T(1024)S(1)} %get-tuple-element.40), kind=kLoop, calls=%fused_computation.7 | loop fusion | flops 22020096 | bytes 22045696 | tf_op jit(solution)/shard_map/convert_element_type | solution.py:411
  305.0 1.7 fusion.24
  307.4 1.8 copy-done.2
  309.2 1.7 multiply_reduce_fusion.1
  312.4 2.6 collective-permute-start.1
  315.0 3.1 fusion.28
  318.2 2.5 fusion.50
  320.6 3.3 collective-permute-start
  324.1 6.2 %fusion.9 = f32[1024,512]{0,1:T(8,128)S(1)} fusion(bf16[1024,2688]{1,0:T(8,128)(2,1)} %copy-done.3, bf16[5376,512]{1,0:T(8,128)(2,1)} %get-tuple-element.13), kind=kOutput, calls=%fused_computation.23 | convolution fusion | flops 2818572288 | bytes 10354688 | tf_op jit(solution)/shard_map/dot_general | solution.py:420
  330.3 6.3 %multiply_reduce_fusion = (f32[1024,4]{0,1:T(4,128)S(1)}, f32[1024,512]{0,1:T(8,128)}) fusion(f32[1024,512]{0,1:T(8,128)S(1)} %fusion.9, bf16[1024,2688]{1,0:T(8,128)(2,1)S(1)} %bitcast.150, bf16[5376,512]{1,0:T(8,128)(2,1)} %get-tuple-element.13), kind=kOutput, calls=%fused_computation.48 | convolution fusion | flops 2820141056 | bytes 12468224 | tf_op jit(solution)/shard_map/dot_general | solution.py:418
  336.8 2.9 fusion.32
  339.8 2.8 fusion.34
  342.5 2.0 multiply_multiply_fusion
  345.9 2.1 fusion.100
  349.9 1.6 fusion.97
  351.5 1.7 fusion.113
  354.2 1.6 fusion.112
  356.9 1.6 fusion.111
  359.5 1.6 fusion.110
  361.7 9.4 %convolution_convert_fusion = bf16[1024,5376]{1,0:T(8,128)(2,1)S(1)} fusion(bf16[5376,512]{1,0:T(8,128)(2,1)} %get-tuple-element.14, bf16[256,512]{0,1:T(8,128)(2,1)S(1)} %bitcast.169, bf16[256,512]{0,1:T(8,128)(2,1)S(1)} %bitcast.168, bf16[256,512]{0,1:T(8,128)(2,1)S(1)} %bitcast.167, bf16[256,512]{0,1:T(8,128)(2,1)S(1)} %bitcast.166), kind=kOutput, calls=%fused_computation.4 | convolution fusion | flops 5646843904 | bytes 17563648 | tf_op jit(solution)/shard_map/dot_general | solution.py:452
  371.1 3.0 dynamic-slice_bitcast_fusion
  374.1 3.0 copy-done
  377.1 9.4 %collective-permute-done.2 = bf16[2,256,5376]{2,1,0:T(8,128)(2,1)} collective-permute-done((bf16[2,256,5376]{2,1,0:T(8,128)(2,1)}, bf16[2,256,5376]{2,1,0:T(8,128)(2,1)}, u32[]{:S(2)}, u32[]{:S(2)}) %collective-permute-start.2) | collective-permute-done | bytes 5505056 | tf_op jit(solution)/shard_map/ppermute | solution.py:167
  386.5 5.5 %fusion.6 = bf16[2,256,5376]{2,1,0:T(8,128)(2,1)S(1)} fusion(bf16[2,256,5376]{2,1,0:T(8,128)(2,1)} %collective-permute-done.2, bf16[2,2,256,5376]{3,2,1,0:T(8,128)(2,1)} %bitcast.146, s32[]{:T(128)S(6)} %select_n.50), kind=kLoop, calls=%fused_computation.12 | loop fusion | flops 11010048 | bytes 16515076 | tf_op jit(solution)/shard_map/convert_element_type | solution.py:179
  392.3 1.5 copy-done.1
  397.7 29.8 %collective-permute-done.3 = bf16[2,128,2688]{2,1,0:T(8,128)(2,1)} collective-permute-done((bf16[2,128,2688]{2,1,0:T(8,128)(2,1)}, bf16[2,128,2688]{2,1,0:T(8,128)(2,1)}, u32[]{:S(2)}, u32[]{:S(2)}) %collective-permute-start.3) | collective-permute-done | bytes 1376288 | tf_op jit(solution)/shard_map/ppermute | solution.py:167
  427.5 2.1 add_convert_fusion
  430.3 1.7 fusion.8
  433.1 13.3 %collective-permute-done.4 = bf16[128,2688]{1,0:T(8,128)(2,1)S(1)} collective-permute-done((bf16[128,2688]{1,0:T(8,128)(2,1)S(1)}, bf16[128,2688]{1,0:T(8,128)(2,1)S(1)}, u32[]{:S(2)}, u32[]{:S(2)}) %collective-permute-start.4) | collective-permute-done | bytes 688160 | tf_op jit(solution)/shard_map/ppermute | solution.py:167
  446.6 1.9 collective-permute-done.6
  (99 shorter events, 17.3 us)
Async XLA Ops:
  292.7 5.8 %copy-start.15 = (f32[5376]{0:T(1024)S(1)}, f32[5376]{0:T(1024)}, u32[]{:S(2)}) copy-start(f32[5376]{0:T(1024)} %param.15) | copy-start | bytes 64516
  298.6 6.4 %copy-start.20 = (bf16[5376,256]{1,0:T(8,128)(2,1)S(1)}, bf16[5376,256]{1,0:T(8,128)(2,1)}, u32[]{:S(2)}) copy-start(bf16[5376,256]{1,0:T(8,128)(2,1)} %get-tuple-element.12) | copy-start | bytes 8257540
  304.9 2.4 copy-start.3
  305.0 4.2 copy-start.2
  309.1 1.7 copy-start.14
  309.1 1.8 copy-start.18
  309.1 2.8 copy-start.16
  310.9 4.0 copy-start.4
  312.3 5.8 %slice-start = ((s8[5505024]{0:T(1024)(128)(4,1)}), s8[4194304]{0:T(1024)(128)(4,1)S(1)}, s32[]{:S(2)}) async-start(s8[5505024]{0:T(1024)(128)(4,1)} %bitcast.147), calls=%async_computation | async-start | bytes 8388608
  312.4 37.5 %collective-permute-start.1 = (bf16[1024,256]{0,1:T(8,128)(2,1)S(1)}, bf16[1024,256]{0,1:T(8,128)(2,1)}, u32[]{:S(2)}, u32[]{:S(2)}) collective-permute-start(bf16[1024,256]{0,1:T(8,128)(2,1)S(1)} %bitcast.151), channel_id=1, source_target_pairs={{0,8},{8,16},{16,24},{1,9},{9,17},{17,25},{2,10},{10,18},{18,26},{... | collective-permute-start | bytes 1572872 | tf_op jit(solution)/shard_map/ppermute | solution.py:20
  315.0 3.2 slice-start.1
  315.0 3.2 copy-start.19
  318.2 12.1 %slice-start.2 = ((s8[5505024]{0:T(1024)(128)(4,1)}), s8[1310720]{0:T(1024)(128)(4,1)S(1)}, s32[]{:S(2)}) async-start(s8[5505024]{0:T(1024)(128)(4,1)} %bitcast.149), calls=%async_computation.2 | async-start | bytes 2621440
  320.6 25.3 %collective-permute-start = (bf16[1024,256]{1,0:T(8,128)(2,1)}, bf16[1024,256]{1,0:T(8,128)(2,1)}, u32[]{:S(2)}, u32[]{:S(2)}) collective-permute-start(bf16[1024,256]{1,0:T(8,128)(2,1)} %fusion.50), channel_id=1, source_target_pairs={{0,8},{8,16},{16,24},{1,9},{9,17},{17,25},{2,10},{10,18},{18,26},{... | collective-permute-start | bytes 1572872 | tf_op jit(solution)/shard_map/ppermute | solution.py:20
  324.1 6.2 %slice-start.3 = ((s8[5505024]{0:T(1024)(128)(4,1)}), s8[4194304]{0:T(1024)(128)(4,1)S(1)}, s32[]{:S(2)}) async-start(s8[5505024]{0:T(1024)(128)(4,1)} %bitcast.149), calls=%async_computation.3 | async-start | bytes 8388608
  330.3 12.2 %copy-start.17 = (f32[128]{0:T(128)S(1)}, f32[128]{0:T(128)}, u32[]{:S(2)}) copy-start(f32[128]{0:T(128)} %param.16) | copy-start | bytes 1540
  349.9 1.6 copy-start.9
  349.9 1.6 copy-start.13
  351.5 1.7 copy-start.6
  353.2 1.0 copy-start.7
  353.2 1.0 copy-start.12
  355.9 1.0 copy-start.8
  355.9 1.0 copy-start.11
  358.6 1.0 copy-start.10
  371.1 6.0 %copy-start = (bf16[1024,5376]{1,0:T(8,128)(2,1)}, bf16[1024,5376]{1,0:T(8,128)(2,1)S(1)}, u32[]{:S(2)}) copy-start(bf16[1024,5376]{1,0:T(8,128)(2,1)S(1)} %convolution_convert_fusion) | copy-start | bytes 33030148
  377.1 9.4 %collective-permute-start.2 = (bf16[2,256,5376]{2,1,0:T(8,128)(2,1)}, bf16[2,256,5376]{2,1,0:T(8,128)(2,1)}, u32[]{:S(2)}, u32[]{:S(2)}) collective-permute-start(bf16[2,256,5376]{2,1,0:T(8,128)(2,1)} %dynamic-slice_bitcast_fusion), channel_id=1, source_target_pairs={{0,2},{2,0},{1,3},{3,1},{4,6},{6,4},{5,7},{7,5},{8,10},{10,8},{9,1... | collective-permute-start | bytes 16515080 | tf_op jit(solution)/shard_map/ppermute | solution.py:167
  392.3 1.5 copy-start.1
  395.0 32.5 %collective-permute-start.3 = (bf16[2,128,2688]{2,1,0:T(8,128)(2,1)}, bf16[2,128,2688]{2,1,0:T(8,128)(2,1)}, u32[]{:S(2)}, u32[]{:S(2)}) collective-permute-start(bf16[2,128,2688]{2,1,0:T(8,128)(2,1)} %constant_dynamic-slice_fusion.1), channel_id=1, source_target_pairs={{0,1},{1,0},{2,3},{3,2},{4,5},{5,4},{6,7},{7,6},{8,9},{9,8},{10,11... | collective-permute-start | bytes 4128776 | tf_op jit(solution)/shard_map/ppermute | solution.py:167
  396.7 33.6 %collective-permute-start.5 = (bf16[128,5376]{1,0:T(8,128)(2,1)}, bf16[128,5376]{1,0:T(8,128)(2,1)}, u32[]{:S(2)}, u32[]{:S(2)}) collective-permute-start(bf16[128,5376]{1,0:T(8,128)(2,1)} %dynamic-slice_bitcast_fusion.1), channel_id=1, source_target_pairs={{0,4},{4,0},{1,5},{5,1},{2,6},{6,2},{3,7},{7,3},{8,12},{12,8},{9,1... | collective-permute-start | bytes 4128776 | tf_op jit(solution)/shard_map/ppermute | solution.py:167
  429.7 16.7 %collective-permute-start.4 = (bf16[128,2688]{1,0:T(8,128)(2,1)S(1)}, bf16[128,2688]{1,0:T(8,128)(2,1)S(1)}, u32[]{:S(2)}, u32[]{:S(2)}) collective-permute-start(bf16[128,2688]{1,0:T(8,128)(2,1)S(1)} %dynamic-slice_bitcast_fusion.2), channel_id=1, source_target_pairs={{0,4},{4,0},{1,5},{5,1},{2,6},{6,2},{3,7},{7,3},{8,12},{12,8},{9,1... | collective-permute-start | bytes 2064392 | tf_op jit(solution)/shard_map/ppermute | solution.py:167
  432.0 16.6 %copy-start.5 = (bf16[256,2688]{1,0:T(8,128)(2,1)S(1)}, bf16[256,2688]{1,0:T(8,128)(2,1)}, u32[]{:S(2)}) copy-start(bf16[256,2688]{1,0:T(8,128)(2,1)} %refs_4_.1) | copy-start | bytes 4128772
  432.0 16.4 %collective-permute-start.6 = (bf16[128,2688]{1,0:T(8,128)(2,1)S(1)}, bf16[128,2688]{1,0:T(8,128)(2,1)S(1)}, u32[]{:S(2)}, u32[]{:S(2)}) collective-permute-start(bf16[128,2688]{1,0:T(8,128)(2,1)S(1)} %constant_dynamic-slice_fusion), channel_id=1, source_target_pairs={{0,1},{1,0},{2,3},{3,2},{4,5},{5,4},{6,7},{7,6},{8,9},{9,8},{10,11... | collective-permute-start | bytes 2064392 | tf_op jit(solution)/shard_map/ppermute | solution.py:167

commit v2 on v1

--- a/solution.py
+++ b/solution.py
@@ -171,12 +171,23 @@
     return lax.dynamic_index_in_dim(array, index, axis, keepdims=False)
 
 
-def reduce_in_plane(terms, width_here):
-    rows = terms.shape[0] // 4
+def along_line(block):
+    planes = lax.axis_size("outer")
+    own = lax.axis_index("outer")
+    up, down = [block], [block]
+    for _ in range(planes - 1):
+        up.append(lax.ppermute(up[-1], "outer", [(i, i + 1) for i in range(planes - 1)]))
+        down.append(lax.ppermute(down[-1], "outer", [(i + 1, i) for i in range(planes - 1)]))
+    return [jnp.where(own >= d, up[d], down[planes - d]) for d in range(1, planes)]
+
+
+def plane_of(d):
+    planes = lax.axis_size("outer")
+    return lax.rem(lax.axis_index("outer") - d + planes, planes)
+
+
+def reduce_in_plane(first, second, width_here):
     mid, low, col = lax.axis_index("mid"), lax.axis_index("low"), lax.axis_index("cols")
-    four = terms.reshape(2, 2, rows, -1)
-    got = flipped(pick(four, 1 - low, 1), "low")
-    chip = (pick(four, low, 1).astype(jnp.float32) + got.astype(jnp.float32)).astype(jnp.bfloat16)
 
     def columns(array, index):
         return lax.dynamic_slice_in_dim(array, index * width_here, width_here, array.ndim - 1)
@@ -184,8 +195,13 @@
     def added(a, b):
         return a.astype(jnp.float32) + b.astype(jnp.float32)
 
-    first, second = chip[:, : rows // 2], chip[:, rows // 2 :]
+    def chip_sum(terms):
+        got = flipped(pick(terms, 1 - low, 1), "low")
+        return added(pick(terms, low, 1), got).astype(jnp.bfloat16)
+
+    first = chip_sum(first)
     got_a = flipped(columns(first, 1 - col), "cols")
+    second = chip_sum(second)
     got_b = flipped(pick(second, 1 - mid, 0), "mid")
     part_a = added(columns(first, col), got_a).astype(jnp.bfloat16)
     part_b = added(pick(second, mid, 0), got_b).astype(jnp.bfloat16)
@@ -196,7 +212,7 @@
     )
 
 
-def gather_kernel(planes, count, *refs):
+def gather_kernel(planes, count, relayed, *refs):
     weights, tokens = refs[:count], refs[count]
     fulls, panel = refs[count + 1 : 2 * count + 1], refs[2 * count + 1]
     (own_sem, deal_send, deal_recv, up_send, up_recv, down_send, down_recv) = refs[
@@ -309,7 +325,7 @@
                         local(t).wait()
                     else:
                         deal(t, k).wait_recv()
-                if d > 0:
+                if d > 0 and k < relayed[t]:
 
                     @pl.when(own - d >= 0)
                     def _():
@@ -319,7 +335,7 @@
                     def _():
                         down(t, d - 1, k).wait_recv()
 
-                if d < planes - 1:
+                if d < planes - 1 and k < relayed[t]:
 
                     @pl.when((own - d >= 0) & has_up)
                     def _():
@@ -335,6 +351,8 @@
     for d in range(planes - 1):
         for k in range(4):
             for t in range(count):
+                if k >= relayed[t]:
+                    continue
 
                 @pl.when((own - d >= 0) & has_up)
                 def _():
@@ -352,7 +370,7 @@
         share(k).wait()
 
 
-def gather_all(weights, tokens):
+def gather_all(weights, tokens, relayed):
     planes = lax.axis_size("outer")
     count = len(weights)
     depth = weights[0].shape[0]
@@ -364,7 +382,7 @@
     ]
     shapes.append(jax.ShapeDtypeStruct((2, 4 * tokens.shape[0], tokens.shape[1]), tokens.dtype))
     return pl.pallas_call(
-        functools.partial(gather_kernel, planes, count),
+        functools.partial(gather_kernel, planes, count, relayed),
         out_shape=shapes,
         in_specs=[anywhere] * (count + 1),
         out_specs=[anywhere] * (count + 1),
@@ -403,8 +421,11 @@
     inner = 4
     plane_tokens = inner * rows_here
     key_full, value_full, query_full, output_full, panel = gather_all(
-        [key_weight, value_weight, query_weight, output_weight.T], activations
-    )
+        [key_weight, value_weight, query_weight, output_weight.T], activations, (4, 4, 4, 0)
+    )
+    own_rows = output_full.shape[0] // lax.axis_size("outer")
+    mine = lax.dynamic_slice_in_dim(output_full, lax.axis_index("outer") * own_rows, own_rows, 0)
+    line = along_line(mine)
     left, right = panel[0].astype(jnp.float32), panel[1].astype(jnp.float32)
     squares = jnp.sum(left * left, axis=-1) + jnp.sum(right * right, axis=-1)
     inverse = lax.rsqrt(squares[:, None] / (2 * width_here) + 1e-06)
@@ -448,11 +469,20 @@
                 key_positions[at : at + count],
             )
         )
-    context = jnp.concatenate(contexts, axis=0)
-    terms = lax.dot_general(
-        context, output_full, (((1,), (1,)), ((), ())), preferred_element_type=jnp.float32
-    ).astype(jnp.bfloat16)
-    summed = reduce_in_plane(terms, width_here)
+    for d in range(1, lax.axis_size("outer")):
+        output_full = lax.dynamic_update_slice_in_dim(
+            output_full, line[d - 1], plane_of(d) * own_rows, 0
+        )
+    half = rows_here // 2
+
+    def projected(at):
+        context = jnp.concatenate([block[at : at + half] for block in contexts], axis=0)
+        terms = lax.dot_general(
+            context, output_full, (((1,), (1,)), ((), ())), preferred_element_type=jnp.float32
+        )
+        return terms.astype(jnp.bfloat16).reshape(2, 2, half, -1)
+
+    summed = reduce_in_plane(projected(0), projected(half), width_here)
     return (activations.astype(jnp.float32) + summed).astype(jnp.bfloat16)
 
 

time: 450 us -> 427 us (0.949)
  Pallas kernels: 292 us -> 204 us
  waiting for transfers between devices: 54.4 us -> 89.6 us
  starting transfers between devices: 9.13 us -> 28.9 us
    pallas_call x1, Pallas kernels: 292 us -> 204 us  [gather_all(): pl.pallas_call(functools.partial(gather_kernel, planes, count, relayed),...]
    ppermute x0 -> x6, waiting for transfers between devices: none -> 43.2 us  [the longest x3 28.8 us: along_line(): lax.ppermute(down[-1], 'outer', [(i + 1, i) for i in range(planes - 1)])]
    ppermute x0 -> x6, starting transfers between devices: none -> 20.2 us  [the longest x3 16.2 us: along_line(): lax.ppermute(up[-1], 'outer', [(i, i + 1) for i in range(planes - 1)])]
    ppermute x5 -> x6, waiting for transfers between devices: 54.4 us -> 46.4 us  [flipped(): return lax.ppermute(value, axis, [(0, 1), (1, 0)])]
    dot_general x1 -> x2, matrix products: 9.41 us -> 7.26 us  [projected(): lax.dot_general(context, output_full, (((1,), (1,)), ((), ())), preferred...]
  transfers between devices with their start and end apart: 7 -> 14, of which waited for: 4 -> 9; matrix products, arithmetic and copies ran while one was open for 8% -> 20% of each run, Pallas kernels for 0% -> 0%
where the time goes in v2:
time: 427 us; the launch traced here: 426 us
  Pallas kernels  204 us (48%)
  waiting for transfers between devices  89.6 us (21%)
  matrix products  43.4 us (10%)
  other arithmetic  39.8 us (9%)
  starting transfers between devices  28.9 us (7%)
  local copies, waits for them, and re-layouts  19.8 us (5%)
    pallas_call x1, Pallas kernels, gather_all(): pl.pallas_call(functools.partial(gather_kernel, planes, count, relayed),...  204 us
    ppermute x6, waiting for transfers between devices, flipped(): return lax.ppermute(value, axis, [(0, 1), (1, 0)])  46.4 us
    ppermute x3, waiting for transfers between devices, along_line(): lax.ppermute(down[-1], 'outer', [(i + 1, i) for i in range(planes - 1)])  28.8 us
    ppermute x3, starting transfers between devices, along_line(): lax.ppermute(up[-1], 'outer', [(i, i + 1) for i in range(planes - 1)])  16.2 us
    ppermute x3, waiting for transfers between devices, along_line(): lax.ppermute(up[-1], 'outer', [(i, i + 1) for i in range(planes - 1)])  14.3 us
    dot_general x3, matrix products, project(): jnp.dot(normed_right, weight[width_here:], preferred_element_type=jnp.flo...  11 us
    dot_general x4, matrix products, attend(): jnp.einsum('qgrd,kgd->grqk', query_four, key_three, preferred_element_typ...  10.6 us
  transfers between devices with their start and end apart: 14, of which 9 were waited for; matrix products, arithmetic and copies ran while one was open for 20% of the time, Pallas kernels for 0%

profile of v2, /device:TPU:0, one launch (start us, length us, event | category | flops | bytes accessed | tf_op | source)
XLA Modules:
  0.0 425.9 jit_solution(16772366496311884586)
XLA Ops:
  0.0 203.7 %gather_weights.1 = (bf16[5376,256]{1,0:T(8,128)(2,1)}, bf16[5376,256]{1,0:T(8,128)(2,1)}, bf16[5376,512]{1,0:T(8,128)(2,1)}, bf16[5376,512]{1,0:T(8,128)(2,1)}, bf16[2,1024,2688]{2,1,0:T(8,128)(2,1)}) custom-call(bf16[336,1024]{1,0:T(8,128)(2,1)} %refs_0_.1, bf16[336,1024]{1,0:T(8,128)(2,1)} %refs_1_.1, bf16[336,2048]{1,0:T(8,128)(2,1)} %refs_2_.1, ...), custom_call_target="tpu_custom_call" | custom-call | flops 199999995904 | bytes 600000000 | tf_op jit(solution)/shard_map/gather_weights/pallas_call | solution.py:384
  203.7 2.5 constant_dynamic-slice_fusion.2
  207.5 5.7 %collective-permute-start.2 = (bf16[1344,512]{1,0:T(8,128)(2,1)}, bf16[1344,512]{1,0:T(8,128)(2,1)}, u32[]{:S(2)}, u32[]{:S(2)}) collective-permute-start(bf16[1344,512]{1,0:T(8,128)(2,1)} %constant_dynamic-slice_fusion.2), channel_id=1, source_target_pairs={{0,8},{8,16},{16,24},{1,9},{9,17},{17,25},{2,10},{10,18},{18,26},{... | collective-permute-start | bytes 4128776 | tf_op jit(solution)/shard_map/ppermute | solution.py:179
  213.2 5.8 %fusion.3 = (f32[1024]{0:T(1024)S(1)}, f32[1024]{0:T(1024)S(1)}) fusion(bf16[2,1024,2688]{2,1,0:T(8,128)(2,1)} %get-tuple-element.10), kind=kLoop, calls=%fused_computation.7 | loop fusion | flops 16513024 | bytes 11018240 | tf_op jit(solution)/shard_map/reduce_sum | solution.py:430
  219.0 6.3 %fusion.2 = (bf16[1024,2688]{1,0:T(8,128)(2,1)S(1)}, bf16[1024,2688]{1,0:T(8,128)(2,1)S(1)}) fusion(f32[2688]{0:T(1024)S(1)} %get-tuple-element.45, f32[1024]{0:T(1024)S(1)} %add_rsqrt_fusion.2, bf16[2,1024,2688]{2,1,0:T(8,128)(2,1)} %get-tuple-element.10, f32[2688]{0:T(1024)S(1)} %get-tuple-element.46), kind=kLoop, calls=%fused_computation.6 | loop fusion | flops 22020096 | bytes 22045696 | tf_op jit(solution)/shard_map/convert_element_type | solution.py:432
  232.8 2.4 collective-permute-start.1
  235.2 3.1 fusion.29
  240.1 3.5 collective-permute-start
  243.8 6.2 %fusion.10 = f32[1024,512]{0,1:T(8,128)S(1)} fusion(bf16[1024,2688]{1,0:T(8,128)(2,1)} %copy-done.2, bf16[5376,512]{1,0:T(8,128)(2,1)} %get-tuple-element.13), kind=kOutput, calls=%fused_computation.27 | convolution fusion | flops 2818572288 | bytes 10354688 | tf_op jit(solution)/shard_map/dot_general | solution.py:441
  250.0 5.0 %multiply_reduce_fusion = (f32[1024,4]{0,1:T(4,128)S(1)}, f32[1024,512]{0,1:T(8,128)S(1)}) fusion(f32[1024,512]{0,1:T(8,128)S(1)} %fusion.10, bf16[1024,2688]{1,0:T(8,128)(2,1)S(1)} %bitcast.161, bf16[5376,512]{1,0:T(8,128)(2,1)} %get-tuple-element.13), kind=kOutput, calls=%fused_computation.52 | convolution fusion | flops 2820141056 | bytes 12468224 | tf_op jit(solution)/shard_map/dot_general | solution.py:439
  256.9 2.8 fusion.33
  259.7 2.9 fusion.35
  262.7 2.8 fusion.91
  265.5 3.1 fusion.122
  272.8 3.2 fusion.78
  277.3 3.0 fusion.123
  283.2 5.8 %collective-permute-start.6 = (bf16[1344,512]{1,0:T(8,128)(2,1)}, bf16[1344,512]{1,0:T(8,128)(2,1)}, u32[]{:S(2)}, u32[]{:S(2)}) collective-permute-start(bf16[1344,512]{1,0:T(8,128)(2,1)} %collective-permute-done.2), channel_id=1, source_target_pairs={{0,8},{8,16},{16,24},{1,9},{9,17},{17,25},{2,10},{10,18},{18,26},{... | collective-permute-start | bytes 4128776 | tf_op jit(solution)/shard_map/ppermute | solution.py:179
  290.2 13.9 %collective-permute-done.4 = bf16[1344,512]{1,0:T(8,128)(2,1)S(1)} collective-permute-done((bf16[1344,512]{1,0:T(8,128)(2,1)}, bf16[1344,512]{1,0:T(8,128)(2,1)S(1)}, u32[]{:S(2)}, u32[]{:S(2)}) %collective-permute-start.4) | collective-permute-done | bytes 1376288 | tf_op jit(solution)/shard_map/ppermute | solution.py:180
  308.4 2.8 fusion.125
  311.7 4.5 %collective-permute-done.6 = bf16[1344,512]{1,0:T(8,128)(2,1)} collective-permute-done((bf16[1344,512]{1,0:T(8,128)(2,1)}, bf16[1344,512]{1,0:T(8,128)(2,1)}, u32[]{:S(2)}, u32[]{:S(2)}) %collective-permute-start.6) | collective-permute-done | bytes 1376288 | tf_op jit(solution)/shard_map/ppermute | solution.py:179
  316.2 4.7 %collective-permute-start.7 = (bf16[1344,512]{1,0:T(8,128)(2,1)}, bf16[1344,512]{1,0:T(8,128)(2,1)S(1)}, u32[]{:S(2)}, u32[]{:S(2)}) collective-permute-start(bf16[1344,512]{1,0:T(8,128)(2,1)} %collective-permute-done.6), channel_id=1, source_target_pairs={{0,8},{8,16},{16,24},{1,9},{9,17},{17,25},{2,10},{10,18},{18,26},{... | collective-permute-start | bytes 4128776 | tf_op jit(solution)/shard_map/ppermute | solution.py:179
  321.0 15.0 %collective-permute-done.5 = bf16[1344,512]{1,0:T(8,128)(2,1)} collective-permute-done((bf16[1344,512]{1,0:T(8,128)(2,1)S(1)}, bf16[1344,512]{1,0:T(8,128)(2,1)}, u32[]{:S(2)}, u32[]{:S(2)}) %collective-permute-start.5) | collective-permute-done | bytes 1376288 | tf_op jit(solution)/shard_map/ppermute | solution.py:180
  338.2 9.8 %collective-permute-done.7 = bf16[1344,512]{1,0:T(8,128)(2,1)S(1)} collective-permute-done((bf16[1344,512]{1,0:T(8,128)(2,1)}, bf16[1344,512]{1,0:T(8,128)(2,1)S(1)}, u32[]{:S(2)}, u32[]{:S(2)}) %collective-permute-start.7) | collective-permute-done | bytes 1376288 | tf_op jit(solution)/shard_map/ppermute | solution.py:179
  349.8 3.6 convolution_convert_fusion.1
  356.7 3.6 convolution_convert_fusion
  364.2 2.6 fusion.7
  369.2 2.5 fusion.6
  373.3 27.2 %collective-permute-done.9 = bf16[2,128,2688]{2,1,0:T(8,128)(2,1)} collective-permute-done((bf16[2,128,2688]{2,1,0:T(8,128)(2,1)}, bf16[2,128,2688]{2,1,0:T(8,128)(2,1)}, u32[]{:S(2)}, u32[]{:S(2)}) %collective-permute-start.9) | collective-permute-done | bytes 1376288 | tf_op jit(solution)/shard_map/ppermute | solution.py:167
  400.5 2.1 add_convert_fusion
  403.0 3.3 collective-permute-done.12
  409.0 11.4 %collective-permute-done.10 = bf16[128,2688]{1,0:T(8,128)(2,1)S(1)} collective-permute-done((bf16[128,2688]{1,0:T(8,128)(2,1)S(1)}, bf16[128,2688]{1,0:T(8,128)(2,1)S(1)}, u32[]{:S(2)}, u32[]{:S(2)}) %collective-permute-start.10) | collective-permute-done | bytes 688160 | tf_op jit(solution)/shard_map/ppermute | solution.py:167
  420.5 3.9 collective-permute-done.13
  (128 shorter events, 46.4 us)
Async XLA Ops:
  206.2 65.0 %collective-permute-start.3 = (bf16[1344,512]{1,0:T(8,128)(2,1)}, bf16[1344,512]{1,0:T(8,128)(2,1)}, u32[]{:S(2)}, u32[]{:S(2)}) collective-permute-start(bf16[1344,512]{1,0:T(8,128)(2,1)} %constant_dynamic-slice_fusion.2), channel_id=1, source_target_pairs={{8,0},{16,8},{24,16},{9,1},{17,9},{25,17},{10,2},{18,10},{26,18},{... | collective-permute-start | bytes 4128776 | tf_op jit(solution)/shard_map/ppermute | solution.py:180
  207.5 75.7 %collective-permute-start.2 = (bf16[1344,512]{1,0:T(8,128)(2,1)}, bf16[1344,512]{1,0:T(8,128)(2,1)}, u32[]{:S(2)}, u32[]{:S(2)}) collective-permute-start(bf16[1344,512]{1,0:T(8,128)(2,1)} %constant_dynamic-slice_fusion.2), channel_id=1, source_target_pairs={{0,8},{8,16},{16,24},{1,9},{9,17},{17,25},{2,10},{10,18},{18,26},{... | collective-permute-start | bytes 4128776 | tf_op jit(solution)/shard_map/ppermute | solution.py:179
  213.2 5.8 %copy-start.16 = (f32[5376]{0:T(1024)S(1)}, f32[5376]{0:T(1024)}, u32[]{:S(2)}) copy-start(f32[5376]{0:T(1024)} %param.15) | copy-start | bytes 64516
  219.0 6.4 %copy-start.20 = (bf16[5376,256]{1,0:T(8,128)(2,1)S(1)}, bf16[5376,256]{1,0:T(8,128)(2,1)}, u32[]{:S(2)}) copy-start(bf16[5376,256]{1,0:T(8,128)(2,1)} %get-tuple-element.12) | copy-start | bytes 8257540
  225.4 4.2 copy-start.1
  231.4 3.9 copy-start.3
  232.7 5.7 %slice-start = ((s8[5505024]{0:T(1024)(128)(4,1)}), s8[4194304]{0:T(1024)(128)(4,1)S(1)}, s32[]{:S(2)}) async-start(s8[5505024]{0:T(1024)(128)(4,1)} %bitcast.158), calls=%async_computation | async-start | bytes 8388608
  232.8 29.9 %collective-permute-start.1 = (bf16[1024,256]{0,1:T(8,128)(2,1)S(1)}, bf16[1024,256]{0,1:T(8,128)(2,1)}, u32[]{:S(2)}, u32[]{:S(2)}) collective-permute-start(bf16[1024,256]{0,1:T(8,128)(2,1)S(1)} %bitcast.166), channel_id=1, source_target_pairs={{0,8},{8,16},{16,24},{1,9},{9,17},{17,25},{2,10},{10,18},{18,26},{... | collective-permute-start | bytes 1572872 | tf_op jit(solution)/shard_map/ppermute | solution.py:20
  238.4 11.6 %slice-start.2 = ((s8[5505024]{0:T(1024)(128)(4,1)}), s8[1310720]{0:T(1024)(128)(4,1)S(1)}, s32[]{:S(2)}) async-start(s8[5505024]{0:T(1024)(128)(4,1)} %bitcast.160), calls=%async_computation.2 | async-start | bytes 2621440
  240.1 28.5 %collective-permute-start = (bf16[1024,256]{1,0:T(8,128)(2,1)S(1)}, bf16[1024,256]{1,0:T(8,128)(2,1)}, u32[]{:S(2)}, u32[]{:S(2)}) collective-permute-start(bf16[1024,256]{1,0:T(8,128)(2,1)S(1)} %fusion.51), channel_id=1, source_target_pairs={{0,8},{8,16},{16,24},{1,9},{9,17},{17,25},{2,10},{10,18},{18,26},{... | collective-permute-start | bytes 1572872 | tf_op jit(solution)/shard_map/ppermute | solution.py:20
  243.8 6.2 %slice-start.3 = ((s8[5505024]{0:T(1024)(128)(4,1)}), s8[4194304]{0:T(1024)(128)(4,1)S(1)}, s32[]{:S(2)}) async-start(s8[5505024]{0:T(1024)(128)(4,1)} %bitcast.160), calls=%async_computation.3 | async-start | bytes 8388608
  250.0 5.0 %copy-start.18 = (f32[128]{0:T(128)S(1)}, f32[128]{0:T(128)}, u32[]{:S(2)}) copy-start(f32[128]{0:T(128)} %param.16) | copy-start | bytes 1540
  271.2 32.9 %collective-permute-start.4 = (bf16[1344,512]{1,0:T(8,128)(2,1)}, bf16[1344,512]{1,0:T(8,128)(2,1)S(1)}, u32[]{:S(2)}, u32[]{:S(2)}) collective-permute-start(bf16[1344,512]{1,0:T(8,128)(2,1)} %collective-permute-done.3), channel_id=1, source_target_pairs={{8,0},{16,8},{24,16},{9,1},{17,9},{25,17},{10,2},{18,10},{26,18},{... | collective-permute-start | bytes 4128776 | tf_op jit(solution)/shard_map/ppermute | solution.py:180
  283.2 22.2 %copy-start.12 = (bf16[256,2,2,128]{0,3,2,1:T(8,128)(2,1)S(1)}, bf16[256,2,2,128]{0,3,2,1:T(8,128)(2,1)}, u32[]{:S(2)}) copy-start(bf16[256,2,2,128]{0,3,2,1:T(8,128)(2,1)} %fusion.78) | copy-start | bytes 786436
  283.2 33.0 %collective-permute-start.6 = (bf16[1344,512]{1,0:T(8,128)(2,1)}, bf16[1344,512]{1,0:T(8,128)(2,1)}, u32[]{:S(2)}, u32[]{:S(2)}) collective-permute-start(bf16[1344,512]{1,0:T(8,128)(2,1)} %collective-permute-done.2), channel_id=1, source_target_pairs={{0,8},{8,16},{16,24},{1,9},{9,17},{17,25},{2,10},{10,18},{18,26},{... | collective-permute-start | bytes 4128776 | tf_op jit(solution)/shard_map/ppermute | solution.py:179
  289.0 19.3 %copy-start.8 = (bf16[1280,256]{0,1:T(8,128)(2,1)S(1)}, bf16[1280,256]{0,1:T(8,128)(2,1)}, u32[]{:S(2)}) copy-start(bf16[1280,256]{0,1:T(8,128)(2,1)} %get-tuple-element.31) | copy-start | bytes 1966084
  304.1 31.9 %collective-permute-start.5 = (bf16[1344,512]{1,0:T(8,128)(2,1)S(1)}, bf16[1344,512]{1,0:T(8,128)(2,1)}, u32[]{:S(2)}, u32[]{:S(2)}) collective-permute-start(bf16[1344,512]{1,0:T(8,128)(2,1)S(1)} %collective-permute-done.4), channel_id=1, source_target_pairs={{8,0},{16,8},{24,16},{9,1},{17,9},{25,17},{10,2},{18,10},{26,18},{... | collective-permute-start | bytes 4128776 | tf_op jit(solution)/shard_map/ppermute | solution.py:180
  308.3 27.6 %slice-start.4 = ((s8[5505024]{0:T(1024)(128)(4,1)}), s8[4194304]{0:T(1024)(128)(4,1)S(1)}, s32[]{:S(2)}) async-start(s8[5505024]{0:T(1024)(128)(4,1)} %bitcast.176), calls=%async_computation.4 | async-start | bytes 8388608
  308.4 27.6 %slice-start.5 = ((s8[5505024]{0:T(1024)(128)(4,1)}), s8[1310720]{0:T(1024)(128)(4,1)S(1)}, s32[]{:S(2)}) async-start(s8[5505024]{0:T(1024)(128)(4,1)} %bitcast.176), calls=%async_computation.5 | async-start | bytes 2621440
  316.2 31.8 %collective-permute-start.7 = (bf16[1344,512]{1,0:T(8,128)(2,1)}, bf16[1344,512]{1,0:T(8,128)(2,1)S(1)}, u32[]{:S(2)}, u32[]{:S(2)}) collective-permute-start(bf16[1344,512]{1,0:T(8,128)(2,1)} %collective-permute-done.6), channel_id=1, source_target_pairs={{0,8},{8,16},{16,24},{1,9},{9,17},{17,25},{2,10},{10,18},{18,26},{... | collective-permute-start | bytes 4128776 | tf_op jit(solution)/shard_map/ppermute | solution.py:179
  338.2 11.6 %copy-start.14 = (bf16[128,2,2,128]{0,3,2,1:T(8,128)(2,1)S(1)}, bf16[128,2,2,128]{0,3,2,1:T(8,128)(2,1)}, u32[]{:S(2)}) copy-start(bf16[128,2,2,128]{0,3,2,1:T(8,128)(2,1)} %get-tuple-element.37) | copy-start | bytes 393220
  353.4 3.3 copy-start.4
  356.7 7.4 %collective-permute-start.8 = (bf16[2,128,5376]{2,1,0:T(8,128)(2,1)}, bf16[2,128,5376]{2,1,0:T(8,128)(2,1)S(1)}, u32[]{:S(2)}, u32[]{:S(2)}) collective-permute-start(bf16[2,128,5376]{2,1,0:T(8,128)(2,1)} %dynamic-slice_bitcast_fusion.1), channel_id=1, source_target_pairs={{0,2},{2,0},{1,3},{3,1},{4,6},{6,4},{5,7},{7,5},{8,10},{10,8},{9,1... | collective-permute-start | bytes 8257544 | tf_op jit(solution)/shard_map/ppermute | solution.py:167
  360.4 3.3 copy-start.5
  363.7 5.6 %collective-permute-start.11 = (bf16[2,128,5376]{2,1,0:T(8,128)(2,1)}, bf16[2,128,5376]{2,1,0:T(8,128)(2,1)}, u32[]{:S(2)}, u32[]{:S(2)}) collective-permute-start(bf16[2,128,5376]{2,1,0:T(8,128)(2,1)} %dynamic-slice_bitcast_fusion), channel_id=1, source_target_pairs={{0,2},{2,0},{1,3},{3,1},{4,6},{6,4},{5,7},{7,5},{8,10},{10,8},{9,1... | collective-permute-start | bytes 8257544 | tf_op jit(solution)/shard_map/ppermute | solution.py:167
  364.2 5.1 %copy-start.6 = (bf16[512,5376]{1,0:T(8,128)(2,1)S(1)}, bf16[512,5376]{1,0:T(8,128)(2,1)}, u32[]{:S(2)}) copy-start(bf16[512,5376]{1,0:T(8,128)(2,1)} %copy-done.5) | copy-start | bytes 16515076
  366.7 5.0 %copy-start = (bf16[2,128,5376]{2,1,0:T(8,128)(2,1)}, bf16[2,128,5376]{2,1,0:T(8,128)(2,1)S(1)}, u32[]{:S(2)}) copy-start(bf16[2,128,5376]{2,1,0:T(8,128)(2,1)S(1)} %fusion.7) | copy-start | bytes 8257540
  368.1 32.4 %collective-permute-start.9 = (bf16[2,128,2688]{2,1,0:T(8,128)(2,1)}, bf16[2,128,2688]{2,1,0:T(8,128)(2,1)}, u32[]{:S(2)}, u32[]{:S(2)}) collective-permute-start(bf16[2,128,2688]{2,1,0:T(8,128)(2,1)} %constant_dynamic-slice_fusion.1), channel_id=1, source_target_pairs={{0,1},{1,0},{2,3},{3,2},{4,5},{5,4},{6,7},{7,6},{8,9},{9,8},{10,11... | collective-permute-start | bytes 4128776 | tf_op jit(solution)/shard_map/ppermute | solution.py:167
  373.0 33.3 %collective-permute-start.12 = (bf16[128,5376]{1,0:T(8,128)(2,1)}, bf16[128,5376]{1,0:T(8,128)(2,1)}, u32[]{:S(2)}, u32[]{:S(2)}) collective-permute-start(bf16[128,5376]{1,0:T(8,128)(2,1)} %dynamic-slice_bitcast_fusion.2), channel_id=1, source_target_pairs={{0,4},{4,0},{1,5},{5,1},{2,6},{6,2},{3,7},{7,3},{8,12},{12,8},{9,1... | collective-permute-start | bytes 4128776 | tf_op jit(solution)/shard_map/ppermute | solution.py:167
  402.6 17.7 %collective-permute-start.10 = (bf16[128,2688]{1,0:T(8,128)(2,1)S(1)}, bf16[128,2688]{1,0:T(8,128)(2,1)S(1)}, u32[]{:S(2)}, u32[]{:S(2)}) collective-permute-start(bf16[128,2688]{1,0:T(8,128)(2,1)S(1)} %dynamic-slice_bitcast_fusion.3), channel_id=1, source_target_pairs={{0,4},{4,0},{1,5},{5,1},{2,6},{6,2},{3,7},{7,3},{8,12},{12,8},{9,1... | collective-permute-start | bytes 2064392 | tf_op jit(solution)/shard_map/ppermute | solution.py:167
  408.0 16.6 %copy-start.7 = (bf16[256,2688]{1,0:T(8,128)(2,1)S(1)}, bf16[256,2688]{1,0:T(8,128)(2,1)}, u32[]{:S(2)}) copy-start(bf16[256,2688]{1,0:T(8,128)(2,1)} %refs_4_.1) | copy-start | bytes 4128772
  408.0 16.4 %collective-permute-start.13 = (bf16[128,2688]{1,0:T(8,128)(2,1)S(1)}, bf16[128,2688]{1,0:T(8,128)(2,1)S(1)}, u32[]{:S(2)}, u32[]{:S(2)}) collective-permute-start(bf16[128,2688]{1,0:T(8,128)(2,1)S(1)} %constant_dynamic-slice_fusion), channel_id=1, source_target_pairs={{0,1},{1,0},{2,3},{3,2},{4,5},{5,4},{6,7},{7,6},{8,9},{9,8},{10,11... | collective-permute-start | bytes 2064392 | tf_op jit(solution)/shard_map/ppermute | solution.py:167
  (9 other events, 20.1 us)
